TPU v7x, 128 devices: a whole 4x4x4 slice. The times are simulated.
128 devices in a mesh: row: 8 (over z_hi, x), col: 16 (over z_lo, y, core).
Axes of the slice: x: 4, y: 4, z: 4 (z_hi: 2, z_lo: 2; z = z_hi * 2 + z_lo), core: 2. Of those that a mesh axis runs over, the one named last changes fastest.
Arguments:
- samples: bfloat16 [262144, 2048], P(('row', 'col')), may hold values from -6 to 6
- prev_factor: float32 [262144, 992], P(('row', 'col')), may hold values from -0.03 to 0.03
- pivots: int32 [32], replicated, may hold values from 0 to 262143, as said below
- inv_diag: float32 [262144], P(('row', 'col')), may hold values from 0.1 to 3
- rhs: float32 [262144], P(('row', 'col')), may hold values from -6 to 6
Outputs:
- new_cols: float32 [262144, 32], P(('row', 'col'))
- solution: float32 [262144], P(('row', 'col'))
Inputs may be any that keep to these rules, and one draw needn't show every extreme that they name: `pivots`: 32 distinct sample indices.
All inputs are finite; a program needn't handle non-finite values.
Results may differ from a plain program's by a relative error of at most 0.0003.
Values sent between devices are 32-bit elements; how exact they have to be, the bound alone decides.
No kernel may reach another device: no remote copies, remote signals or barrier semaphores. Data moves between devices by JAX's collectives and lax.ppermute only.
A program may use at most 128 MiB of HBM per device.

v0:
```python
import functools

import jax
import jax.numpy as jnp
from jax import lax
from jax.experimental import pallas as pl
from jax.experimental.pallas import tpu as pltpu
from jax.sharding import PartitionSpec as P

FEAT = 2048
PREV = 992
PANEL = 32
RANK = 1024
ROWS = 2048
LANES = 128
NB = RANK // LANES
PACKED = [PREV - j * LANES for j in range(NB)]
PACKED_AT = [sum(PACKED[:j]) for j in range(NB + 1)]
GRAM_ROWS = PACKED_AT[NB]
PICK_ROWS = PANEL * (FEAT + RANK) // LANES
SEND_ROWS = GRAM_ROWS + PICK_ROWS
HALF = SEND_ROWS // 2
EXT = 40
EXT_ROWS = 512
HIGHEST = lax.Precision.HIGHEST
F32 = jnp.float32
BF16 = jnp.bfloat16
AXES = ("row", "col")
VMEM_LIMIT = 50 * 2**20


def split(x):
    high = x.astype(BF16)
    return high, (x - high.astype(F32)).astype(BF16)


def three(x):
    high = x.astype(BF16)
    rest = x - high.astype(F32)
    mid = rest.astype(BF16)
    return high, mid, (rest - mid.astype(F32)).astype(BF16)


def mm(a, b, dims, precision=None):
    return lax.dot_general(a, b, (dims, ((), ())), precision=precision, preferred_element_type=F32)


NN = ((1,), (0,))
NT = ((1,), (1,))


def column(row):
    return jnp.broadcast_to(row, (LANES, LANES)).T


def whole(i):
    return (0, 0)


def by_half(start, stop):
    cuts = [start] + [HALF] * (start < HALF < stop) + [stop]
    return [(a // HALF, a % HALF, a - start, b - a) for a, b in zip(cuts, cuts[1:])]


GRAM_TILE = 1024


def gram_kernel(pivots_ref, place_ref, diag_ref, samples_ref, prev_ref, keep_ref, send_ref, acc_ref, picks_ref, srow_ref, sem):
    step = pl.program_id(0)
    base = place_ref[0]

    def row_copy(p):
        start = pl.multiple_of((pivots_ref[p] - base) // 16 * 16, 16)
        return pltpu.make_async_copy(samples_ref.at[pl.ds(start, 16)], srow_ref.at[p], sem.at[p])

    def owned(p):
        place = pivots_ref[p] - base
        return (place >= 0) & (place < ROWS)

    @pl.when(step == 0)
    def _():
        acc_ref[...] = jnp.zeros_like(acc_ref)
        picks_ref[...] = jnp.zeros_like(picks_ref)

        def start(p, carry):
            @pl.when(owned(p))
            def _():
                row_copy(p).start()

            return carry

        lax.fori_loop(0, PANEL, start, 0)

    high, low = split(prev_ref[...] * jnp.sqrt(diag_ref[...]))
    at = 0
    for j in range(4):
        first = 256 * j
        wide = min(256, PREV - first)
        mine_h, mine_l = high[first : first + wide], low[first : first + wide]
        total = mm(high[first:], mine_h, NT) + (mm(high[first:], mine_l, NT) + mm(low[first:], mine_h, NT))
        acc_ref[at : at + PREV - first, :wide] += total
        at += PREV - first

    def factor_row(p, carry):
        place = pivots_ref[p] - base

        @pl.when(owned(p) & (place // GRAM_TILE == step))
        def _():
            local = place % GRAM_TILE
            start = pl.multiple_of(local // LANES * LANES, LANES)
            chosen = lax.broadcasted_iota(jnp.int32, (16, LANES), 1) == local % LANES
            chosen = jnp.where(chosen, 1.0, 0.0).astype(BF16)
            parts = three(prev_ref[:, pl.ds(start, LANES)])
            row = (mm(chosen, parts[0], NT) + mm(chosen, parts[1], NT) + mm(chosen, parts[2], NT))[:1]
            to = PANEL * FEAT // LANES
            for c in range(NB - 1):
                picks_ref[pl.ds(to + c * PANEL + p, 1), :] = row[:, c * LANES : (c + 1) * LANES]
            picks_ref[pl.ds(to + (NB - 1) * PANEL + p, 1), : PREV % LANES] = row[:, (NB - 1) * LANES :]

        return carry

    lax.fori_loop(0, PANEL, factor_row, 0)

    @pl.when(step == ROWS // GRAM_TILE - 1)
    def _():
        def sample_row(p, carry):
            @pl.when(owned(p))
            def _():
                row_copy(p).wait()
                sub = lax.broadcasted_iota(jnp.int32, (16, FEAT), 0)
                row = jnp.sum(jnp.where(sub == (pivots_ref[p] - base) % 16, srow_ref[p].astype(F32), 0.0), axis=0, keepdims=True)
                for c in range(FEAT // LANES):
                    picks_ref[pl.ds(c * PANEL + p, 1), :] = row[:, c * LANES : (c + 1) * LANES]

            return carry

        lax.fori_loop(0, PANEL, sample_row, 0)

        def write(halves):
            at = 0
            for j in range(NB):
                lane = (j % 2) * LANES
                wide = min(LANES, PREV - j * LANES)
                for half, to, skip, n in by_half(PACKED_AT[j], PACKED_AT[j + 1]):
                    halves[half][to : to + n, :wide] = acc_ref[at + lane + skip : at + lane + skip + n, lane : lane + wide]
                    if wide < LANES:
                        halves[half][to : to + n, wide:] = jnp.zeros((n, LANES - wide), F32)
                at += (PREV - j * LANES + LANES) * (j % 2)
            halves[1][GRAM_ROWS - HALF :, :] = picks_ref[...]

        @pl.when(place_ref[1] == 0)
        def _():
            write((keep_ref, send_ref))

        @pl.when(place_ref[1] == 1)
        def _():
            write((send_ref, keep_ref))


def gram(samples, prev_t, pivots, diag, place):
    half = jax.ShapeDtypeStruct((HALF, LANES), F32)
    return pl.pallas_call(
        gram_kernel,
        grid=(ROWS // GRAM_TILE,),
        out_shape=(half, half),
        in_specs=[
            pl.BlockSpec(memory_space=pltpu.SMEM),
            pl.BlockSpec(memory_space=pltpu.SMEM),
            pl.BlockSpec((1, GRAM_TILE), lambda i: (0, i)),
            pl.BlockSpec(memory_space=pl.ANY),
            pl.BlockSpec((PREV, GRAM_TILE), lambda i: (0, i)),
        ],
        out_specs=(pl.BlockSpec((HALF, LANES), whole), pl.BlockSpec((HALF, LANES), whole)),
        scratch_shapes=[
            pltpu.VMEM((sum(PREV - 256 * j for j in range(4)), 256), F32),
            pltpu.VMEM((PICK_ROWS, LANES), F32),
            pltpu.VMEM((PANEL, 16, FEAT), BF16),
            pltpu.SemaphoreType.DMA((PANEL,)),
        ],
        compiler_params=pltpu.CompilerParams(vmem_limit_bytes=VMEM_LIMIT),
        cost_estimate=pl.CostEstimate(flops=6 * ROWS * RANK * 640, bytes_accessed=ROWS * PREV * 4, transcendentals=0),
        name="gram",
    )(pivots, place, diag, samples, prev_t)


PANEL_TILE = 512


def panel_kernel(place_ref, mine_ref, other_ref, diag_ref, rhs_ref, samples_ref, prev_ref, new_ref, ext_ref, picked_ref, pfac_ref, norm_ref, inv_ref, acc_ref):
    step = pl.program_id(0)
    nfeat = FEAT // LANES

    def prepare(picks_ref):
        def pick(c):
            return picks_ref[GRAM_ROWS - HALF + c * PANEL : GRAM_ROWS - HALF + (c + 1) * PANEL, :]

        acc_ref[...] = jnp.zeros_like(acc_ref)
        picked = jnp.concatenate([pick(c) for c in range(nfeat)], axis=1)
        pfac = jnp.concatenate([pick(nfeat + c) for c in range(NB)], axis=1)[:, :PREV]
        picked16 = picked.astype(BF16)
        picked_ref[...] = picked16
        high, low = split(pfac)
        pfac_ref[:PANEL, :] = high
        pfac_ref[PANEL:, :] = low
        square = picked * picked
        norm_row = mm(jnp.ones((8, FEAT), F32), square, NT, HIGHEST)[:1]
        norm_col = jnp.sum(square, axis=1, keepdims=True)
        norm_ref[...] = jnp.broadcast_to(norm_col, (PANEL, LANES))
        cross = mm(picked16, picked16, NT)
        dist = jnp.maximum(norm_col + norm_row - 2.0 * cross, 0.0)
        a = jnp.exp(-(2.0 / FEAT) * dist) - mm(pfac, pfac, NT, HIGHEST)
        sub = lax.broadcasted_iota(jnp.int32, (PANEL, PANEL), 0)
        lane = lax.broadcasted_iota(jnp.int32, (PANEL, PANEL), 1)
        b = jnp.where(sub == lane, 1.0, 0.0)
        for k in range(PANEL - 1):
            factor = jnp.where(sub > k, a[:, k : k + 1] / a[k : k + 1, k : k + 1], 0.0)
            a, b = a - factor * a[k : k + 1, :], b - factor * b[k : k + 1, :]
        pivot = jnp.sum(jnp.where(sub == lane, a, 0.0), axis=1, keepdims=True)
        inv_ref[...] = b / jnp.sqrt(pivot)

    @pl.when((step == 0) & (place_ref[1] == 1))
    def _():
        prepare(mine_ref)

    @pl.when((step == 0) & (place_ref[1] == 0))
    def _():
        prepare(other_ref)

    tile = samples_ref[...]
    squares = None
    for c in range(nfeat):
        part = tile[:, c * LANES : (c + 1) * LANES].astype(F32)
        squares = part * part if squares is None else squares + part * part
    norm = jnp.concatenate(
        [jnp.sum(squares[c : c + LANES].T, axis=0, keepdims=True) for c in range(0, PANEL_TILE, LANES)], axis=1
    )
    cross = mm(picked_ref[...], tile, NT)
    dist = jnp.maximum(norm + norm_ref[:, :1] - 2.0 * cross, 0.0)
    high, low = split(prev_ref[...])
    both = mm(pfac_ref[...], high, NN)
    inner = both[:PANEL] + (both[PANEL:] + mm(pfac_ref[:PANEL, :], low, NN))
    resid = jnp.exp(-(2.0 / FEAT) * dist) - inner
    new = mm(inv_ref[...], resid, NN, HIGHEST)
    new_ref[...] = new
    sub = lax.broadcasted_iota(jnp.int32, (EXT - PANEL, PANEL_TILE), 0)
    x = diag_ref[...] * jnp.concatenate([new, jnp.where(sub == 0, rhs_ref[...], 0.0)], axis=0)
    x = jnp.concatenate([x, jnp.zeros((48 - EXT, PANEL_TILE), F32)], axis=0)
    xh, xl = split(x)
    nh, nl = split(new)
    high, low = jnp.concatenate([high, nh], axis=0), jnp.concatenate([low, nl], axis=0)
    both = mm(jnp.concatenate([xh, xl], axis=0), high, NT)
    acc_ref[...] += both[:EXT] + (both[48 : 48 + EXT] + mm(xh, low, NT)[:EXT])

    @pl.when(step == ROWS // PANEL_TILE - 1)
    def _():
        for c in range(NB):
            ext_ref[EXT * c : EXT * (c + 1), :] = acc_ref[:, c * LANES : (c + 1) * LANES]
        ext_ref[EXT * NB :, :] = jnp.zeros((EXT_ROWS - EXT * NB, LANES), F32)


def panel(place, mine, other, diag, rhs, samples, prev_t):
    vec = pl.BlockSpec((1, PANEL_TILE), lambda i: (0, i))
    return pl.pallas_call(
        panel_kernel,
        grid=(ROWS // PANEL_TILE,),
        out_shape=(jax.ShapeDtypeStruct((PANEL, ROWS), F32), jax.ShapeDtypeStruct((EXT_ROWS, LANES), F32)),
        in_specs=[
            pl.BlockSpec(memory_space=pltpu.SMEM),
            pl.BlockSpec((HALF, LANES), whole),
            pl.BlockSpec((HALF, LANES), whole),
            vec,
            vec,
            pl.BlockSpec((PANEL_TILE, FEAT), lambda i: (i, 0)),
            pl.BlockSpec((PREV, PANEL_TILE), lambda i: (0, i)),
        ],
        out_specs=(pl.BlockSpec((PANEL, PANEL_TILE), lambda i: (0, i)), pl.BlockSpec((EXT_ROWS, LANES), whole)),
        scratch_shapes=[
            pltpu.VMEM((PANEL, FEAT), BF16),
            pltpu.VMEM((2 * PANEL, PREV), BF16),
            pltpu.VMEM((PANEL, LANES), F32),
            pltpu.VMEM((PANEL, PANEL), F32),
            pltpu.VMEM((EXT, RANK), F32),
        ],
        compiler_params=pltpu.CompilerParams(vmem_limit_bytes=VMEM_LIMIT),
        cost_estimate=pl.CostEstimate(flops=2 * ROWS * RANK * 1000, bytes_accessed=ROWS * (FEAT * 2 + PREV * 4), transcendentals=0),
        name="panel",
    )(place, mine, other, diag, rhs, samples, prev_t)


def inverse8(cols):
    sub = lax.broadcasted_iota(jnp.int32, (8, LANES), 0)

    def row(x, r):
        return jnp.broadcast_to(x[r : r + 1, :], (8, LANES))

    cols = list(cols)
    for k in range(0, 8, 2):
        a, b, c = row(cols[k], k), row(cols[k + 1], k), row(cols[k + 1], k + 1)
        scale = 1.0 / (a * c - b * b)
        ia, ib, ic = c * scale, -b * scale, a * scale
        ua = cols[k] * ia + cols[k + 1] * ib
        ub = cols[k] * ib + cols[k + 1] * ic
        keep = (sub != k) & (sub != k + 1)
        first = sub == k
        for m in range(8):
            if m in (k, k + 1):
                continue
            x, y = row(cols[m], k), row(cols[m], k + 1)
            cols[m] = jnp.where(keep, cols[m] - (ua * x + ub * y), jnp.where(first, ia * x + ib * y, ib * x + ic * y))
        cols[k] = jnp.where(keep, -ua, jnp.where(first, ia, ib))
        cols[k + 1] = jnp.where(keep, -ub, jnp.where(first, ib, ic))
    return cols


def tree(terms):
    while len(terms) > 1:
        terms = [a + b for a, b in zip(terms[::2], terms[1::2])]
    return terms[0]


def inverse128(rows):
    lane = lax.broadcasted_iota(jnp.int32, (8, LANES), 1)
    sub = lax.broadcasted_iota(jnp.int32, (8, LANES), 0)
    rows = list(rows)
    n = len(rows)

    def spread(x, at):
        return jnp.broadcast_to(x[:, at : at + 1], (8, LANES))

    for p in range(n):
        inside = (lane >= 8 * p) & (lane < 8 * p + 8)
        cols = inverse8([spread(rows[p], 8 * p + j) for j in range(8)])
        own = jnp.where(inside, jnp.where(lane == sub + 8 * p, 1.0, 0.0), rows[p])
        pivot = tree([cols[j] * jnp.broadcast_to(own[j : j + 1, :], (8, LANES)) for j in range(8)])
        spread_rows = [jnp.broadcast_to(pivot[j : j + 1, :], (8, LANES)) for j in range(8)]
        rows[p] = pivot
        for step in range(1, n):
            q = (p + step) % n
            update = tree([spread(rows[q], 8 * p + j) * spread_rows[j] for j in range(8)])
            rows[q] = jnp.where(inside, 0.0, rows[q]) - update
        yield
    return rows


EXTRA = EXT - PANEL


def left_parts(x):
    h, m, lo = three(x)
    return jnp.concatenate([h, m], axis=1), jnp.concatenate([h, lo], axis=1)


def right_parts(x, axis):
    h, m, lo = three(x)
    return tuple(jnp.concatenate(pair, axis=axis) for pair in ((h, h), (m, m), (lo, h)))


def product(left, right, dims):
    return mm(left[0], right[0], dims) + (mm(left[0], right[1], dims) + mm(left[1], right[2], dims))


def run(steps, fillers):
    count = LANES // 8
    done = 0
    for i in range(count + 1):
        try:
            next(steps)
        except StopIteration as end:
            for filler in fillers[done:]:
                filler()
            return end.value
        upto = len(fillers) * (i + 1) // count
        for filler in fillers[done:upto]:
            filler()
        done = upto


def eliminate(first, last, cols, t_refs, inv_ref):
    fillers = []
    for k in range(first, last):
        ref, at = cols[k]
        n = PACKED[k] - LANES
        block = run(inverse128([ref[at + 8 * i : at + 8 * i + 8, :] for i in range(LANES // 8)]), fillers)
        block = jnp.concatenate(block, axis=0)
        inv_ref[(k - first) * LANES : (k - first + 1) * LANES, :] = block
        weights = right_parts(block, 0)
        near = min(LANES, n)
        below = ref[at + LANES : at + LANES + near, :]
        right_near = right_parts(below, 1)
        times = product(left_parts(below), weights, NN)
        t_refs[k][:near, :] = times
        next_ref, next_at = cols[k + 1]
        next_ref[next_at : next_at + near, :near] -= product(left_parts(times), right_near, NT)
        fillers = []
        if n == near:
            continue
        far = {}

        def others(ref=ref, at=at, n=n, t_ref=t_refs[k], weights=weights, far=far):
            below = ref[at + 2 * LANES : at + LANES + n, :]
            times = product(left_parts(below), weights, NN)
            t_ref[LANES:, :] = times
            far["left"] = left_parts(times)
            far["right"] = right_parts(below, 1)

        def beside(ref=next_ref, at=next_at, n=n, far=far, right=right_near):
            ref[at + LANES : at + n, :] -= product(far["left"], right, NT)

        def update(j, k=k, n=n, far=far):
            r = (j - k - 2) * LANES
            wide = min(2 * LANES, n - LANES - r)
            value = product(tuple(x[r:] for x in far["left"]), tuple(x[r : r + wide] for x in far["right"]), NT)
            for c in range(0, wide, LANES):
                to_ref, to = cols[j + c // LANES]
                w = min(LANES, wide - c)
                to_ref[to : to + n - LANES - r - c, :w] -= value[c:, c : c + w]

        fillers = [others, beside] + [functools.partial(update, j) for j in range(k + 2, NB, 2)]
    for filler in fillers:
        filler()


CUTS = (0, 4, 7)
LEFT = [PACKED_AT[j] - PACKED_AT[CUTS[1]] for j in range(CUTS[1], NB + 1)]


def solve_first_kernel(place_ref, mine_ref, other_ref, left_ref, inv_ref, *refs):
    t_refs, a_ref = refs[:-1], refs[-1]
    lane = lax.broadcasted_iota(jnp.int32, (LANES, LANES), 1)
    sub = lax.broadcasted_iota(jnp.int32, (LANES, LANES), 0)

    def load(halves):
        for half, at, to, n in by_half(0, PACKED_AT[CUTS[1]]):
            a_ref[to : to + n, :] = halves[half][at : at + n, :]
        for half, at, to, n in by_half(PACKED_AT[CUTS[1]], GRAM_ROWS):
            left_ref[to : to + n, :] = halves[half][at : at + n, :]

    @pl.when(place_ref[1] == 0)
    def _():
        load((mine_ref, other_ref))

    @pl.when(place_ref[1] == 1)
    def _():
        load((other_ref, mine_ref))

    cols = [(a_ref, PACKED_AT[j]) for j in range(CUTS[1])] + [(left_ref, LEFT[j - CUTS[1]]) for j in range(CUTS[1], NB)]
    for j, (ref, at) in enumerate(cols):
        n = min(LANES, PACKED[j])
        ref[at : at + n, :] += jnp.where(lane == sub, 1.0, 0.0)[:n]
    eliminate(0, CUTS[1], cols, dict(enumerate(t_refs)), inv_ref)


def solve_second_kernel(left_ref, last_ref, inv_ref, *refs):
    t_refs, a_ref = refs[:-1], refs[-1]
    a_ref[...] = left_ref[...]
    eliminate(CUTS[1], CUTS[2], {j: (a_ref, LEFT[j - CUTS[1]]) for j in range(CUTS[1], NB)}, {CUTS[1] + i: r for i, r in enumerate(t_refs)}, inv_ref)
    last_ref[...] = a_ref[LEFT[-2] :, :]


def solve_last_kernel(last_ref, inv0_ref, inv1_ref, ext_ref, diag_ref, rhs_ref, new_ref, prev_any, *refs):
    t_refs, (out_ref, e_ref, w_ref, prev_ref, sem) = refs[: NB - 1], refs[NB - 1 :]
    step = PREV // 4
    copies = [pltpu.make_async_copy(prev_any.at[pl.ds(i * step, step)], prev_ref.at[pl.ds(i * step, step)], sem.at[i]) for i in range(4)]
    for copy in copies:
        copy.start()
    tail = PREV % LANES
    for j in range(NB):
        e_ref[:, j * LANES : (j + 1) * LANES] = ext_ref[EXT * j : EXT * (j + 1), :]
    scaled = []
    for k in range(NB - 1):
        here = e_ref[:, k * LANES : (k + 1) * LANES]
        left = left_parts(here)
        n = PACKED[k] - LANES
        change = product(left, right_parts(t_refs[k][...], 1), NT)
        e_ref[:, (k + 1) * LANES : PREV] -= change
        inv = inv0_ref[k * LANES : (k + 1) * LANES, :] if k < CUTS[1] else inv1_ref[(k - CUTS[1]) * LANES : (k - CUTS[1] + 1) * LANES, :]
        times = product(left, right_parts(inv, 0), NN)
        scaled.append(times)
        corner = product(left, right_parts(times, 1), NT)
        total = corner if k == 0 else total + corner
    lane = lax.broadcasted_iota(jnp.int32, (LANES, LANES), 1)
    sub = lax.broadcasted_iota(jnp.int32, (LANES, LANES), 0)
    shifted = jnp.concatenate([jnp.zeros((EXT, tail), F32), total[:, :PANEL]], axis=1)
    bottom = e_ref[:, (NB - 1) * LANES :] - shifted
    bottom = bottom + jnp.where(lax.broadcasted_iota(jnp.int32, (EXT, LANES), 1) == lax.broadcasted_iota(jnp.int32, (EXT, LANES), 0) + tail, 1.0, 0.0)
    block = jnp.concatenate([last_ref[...], bottom[:PANEL]], axis=0)
    block = jnp.where((lane >= tail) & (sub < tail), block.T, block)
    inverse = run(inverse128([block[8 * i : 8 * i + 8, :] for i in range(LANES // 8)]), [])
    inverse = jnp.concatenate(inverse, axis=0)
    value = mm(bottom[PANEL:], inverse, NN, HIGHEST)
    sums = [None] * (NB - 1)
    for k in reversed(range(1, NB)):
        spread = column(value[:1])
        w_ref[k * LANES : (k + 1) * LANES, :] = spread
        for j in range(k):
            r = (k - j - 1) * LANES
            rows = t_refs[j][r : r + min(LANES, PREV - k * LANES), :]
            if k == NB - 1:
                rows = jnp.concatenate([rows, scaled[j][:PANEL]], axis=0)
            part = (rows * spread).reshape(LANES // 8, 8, LANES).sum(axis=0)
            sums[j] = part if sums[j] is None else sums[j] + part
        value = scaled[k - 1][PANEL:] - jnp.sum(sums[k - 1], axis=0, keepdims=True)


    w_ref[:LANES, :] = column(value[:1])

    def weigh(ref, at, to):
        return ref[pl.ds(at, 8), :] * jnp.concatenate([w_ref[pl.ds(to, 8), :]] * (ROWS // LANES), axis=1)

    total = tree([weigh(new_ref, 8 * i, PREV + 8 * i) for i in range(PANEL // 8)])
    for copy in copies:
        copy.wait()

    def some(i, total):
        at = pl.multiple_of(i * 32, 32)
        return total + tree([weigh(prev_ref, at + 8 * j, at + 8 * j) for j in range(4)])

    total = lax.fori_loop(0, PREV // 32, some, total)
    fw = jnp.sum(total, axis=0, keepdims=True)
    out_ref[...] = diag_ref[...] * rhs_ref[...] - diag_ref[...] * fw


def block_spec(rows):
    return pl.BlockSpec((rows, LANES), whole)


def shape(rows):
    return jax.ShapeDtypeStruct((rows, LANES), F32)


def solve_first(place, mine, other):
    below = [PACKED[k] - LANES for k in range(CUTS[1])]
    outs = [LEFT[-1], CUTS[1] * LANES] + below
    return pl.pallas_call(
        solve_first_kernel,
        grid=(1,),
        out_shape=tuple(shape(r) for r in outs),
        in_specs=[pl.BlockSpec(memory_space=pltpu.SMEM), block_spec(HALF), block_spec(HALF)],
        out_specs=tuple(block_spec(r) for r in outs),
        scratch_shapes=[pltpu.VMEM((PACKED_AT[CUTS[1]], LANES), F32)],
        compiler_params=pltpu.CompilerParams(vmem_limit_bytes=VMEM_LIMIT),
        cost_estimate=pl.CostEstimate(flops=2 * 10**10, bytes_accessed=10**7, transcendentals=0),
        name="solve_first",
    )(place, mine, other)


def solve_second(left):
    below = [PACKED[k] - LANES for k in range(CUTS[1], CUTS[2])]
    outs = [PACKED[NB - 1], (CUTS[2] - CUTS[1]) * LANES] + below
    return pl.pallas_call(
        solve_second_kernel,
        grid=(1,),
        out_shape=tuple(shape(r) for r in outs),
        in_specs=[block_spec(LEFT[-1])],
        out_specs=tuple(block_spec(r) for r in outs),
        scratch_shapes=[pltpu.VMEM((LEFT[-1], LANES), F32)],
        compiler_params=pltpu.CompilerParams(vmem_limit_bytes=VMEM_LIMIT),
        cost_estimate=pl.CostEstimate(flops=2 * 10**10, bytes_accessed=10**7, transcendentals=0),
        name="solve_second",
    )(left)


def solve_last(last, inv0, inv1, ext, t, diag, rhs, new_t, prev_t):
    ins = [PACKED[NB - 1], CUTS[1] * LANES, (CUTS[2] - CUTS[1]) * LANES, EXT_ROWS]
    below = [PACKED[k] - LANES for k in range(NB - 1)]
    vec = pl.BlockSpec((1, ROWS), whole)
    return pl.pallas_call(
        solve_last_kernel,
        grid=(1,),
        out_shape=jax.ShapeDtypeStruct((1, ROWS), F32),
        in_specs=[block_spec(r) for r in ins]
        + [vec, vec, pl.BlockSpec((PANEL, ROWS), whole), pl.BlockSpec(memory_space=pl.ANY)]
        + [block_spec(r) for r in below],
        out_specs=vec,
        scratch_shapes=[
            pltpu.VMEM((EXT, RANK), F32),
            pltpu.VMEM((RANK, LANES), F32),
            pltpu.VMEM((PREV, ROWS), F32),
            pltpu.SemaphoreType.DMA((4,)),
        ],
        compiler_params=pltpu.CompilerParams(vmem_limit_bytes=VMEM_LIMIT),
        name="solve_last",
    )(last, inv0, inv1, ext, diag, rhs, new_t, prev_t, *t)


SAME_CORE = [[i for i in range(128) if i % 2 == core] for core in range(2)]
OTHER_CORE = [(i, i ^ 1) for i in range(128)]


def sum_large(keep, send):
    shape = keep.shape
    keep = (keep + lax.ppermute(send, AXES, OTHER_CORE)).reshape(64, -1, LANES)
    parts = lax.all_to_all(keep, AXES, 0, 0, axis_index_groups=SAME_CORE)
    part = jnp.sum(parts, axis=0)
    mine = lax.all_to_all(jnp.broadcast_to(part, parts.shape), AXES, 0, 0, axis_index_groups=SAME_CORE)
    mine = mine.reshape(shape)
    return mine, lax.ppermute(mine, AXES, OTHER_CORE)


def on_device(samples, prev_factor, pivots, inv_diag, rhs):
    index = lax.axis_index(AXES)
    place = jnp.stack([index * ROWS, index % 2]).astype(jnp.int32)
    diag, rhs = inv_diag.reshape(1, ROWS), rhs.reshape(1, ROWS)
    prev_t = prev_factor.T
    keep, send = gram(samples, prev_t, pivots, diag, place)
    mine, other = sum_large(keep, send)
    new_t, ext = panel(place, mine, other, diag, rhs, samples, prev_t)
    parts = lax.all_to_all(ext.reshape(128, -1, LANES), AXES, 0, 0)
    left, inv0, *t0 = solve_first(place, mine, other)
    parts, left = lax.optimization_barrier((parts, left))
    part = jnp.sum(parts, axis=0)
    ext = lax.all_to_all(jnp.broadcast_to(part, parts.shape), AXES, 0, 0).reshape(ext.shape)
    last, inv1, *t1 = solve_second(left)
    out = solve_last(last, inv0, inv1, ext, t0 + t1, diag, rhs, new_t, prev_t)
    return (new_t.T, out.reshape(ROWS))


def solution(mesh):
    return jax.shard_map(
        on_device,
        mesh=mesh,
        in_specs=(
            P(AXES, None),
            P(AXES, None),
            P(),
            P(AXES),
            P(AXES),
        ),
        out_specs=(P(AXES, None), P(AXES)),
        check_vma=False,
    )
```

profile of v0, /device:TPU:1, one launch (start us, length us, event | category | flops | bytes accessed | tf_op | source)
XLA Modules:
  0.0 173.1 jit_solution(4417061409025569513)
XLA Ops:
  0.6 0.1 pad_add_fusion.place_ref
  0.7 0.0 copy-start.2
  0.7 0.7 copy-done.2
  1.4 0.0 copy-start.5
  1.4 0.7 copy-done.5
  2.1 13.8 %gram.1 = (f32[2560,128]{1,0:T(8,128)S(1)}, f32[2560,128]{1,0:T(8,128)S(1)}) custom-call(s32[32]{0:T(128)S(1)} %copy-done.5, s32[2]{0:T(128)S(1)} %pad_add_fusion.place_ref, f32[1,2048]{1,0:T(1,128)S(1)} %bitcast.16, bf16[2048,2048]{1,0:T(8,128)(2,1)} %samples_ref.3, f32[992,2048]{1,0:T(8,128)} %bitcast.21), custom_call_target="tpu_custom_call" | custom-call | flops 8053063680 | bytes 8126464 | tf_op jit(solution)/shard_map/gram/pallas_call | solution.py:162
  15.8 1.2 collective-permute-start
  17.0 2.7 %collective-permute-done = f32[2560,128]{1,0:T(8,128)S(1)} collective-permute-done((f32[2560,128]{1,0:T(8,128)S(1)}, f32[2560,128]{1,0:T(8,128)S(1)}, u32[]{:S(2)}, u32[]{:S(2)}) %collective-permute-start) | collective-permute-done | bytes 1310752 | tf_op jit(solution)/shard_map/ppermute | solution.py:592
  19.7 0.1 add.12
  19.8 30.8 %all_to_all.20 = f32[64,40,128]{2,1,0:T(8,128)S(1)} all-to-all(f32[64,40,128]{2,1,0:T(8,128)S(1)} %bitcast.24), channel_id=1, replica_groups={{0,2,4,6,8,10,12,14,16,18,20,22,24,26,28,30,32,34,36,38,40,42,44,46,48,..., dimensions={0} | all-to-all | bytes 2621440 | tf_op jit(solution)/shard_map/all_to_all | solution.py:593
  50.6 0.1 reduce_sum.18
  50.7 0.1 broadcast_in_dim.6
  50.8 0.0 copy-start.3
  50.8 0.0 copy-start.4
  50.8 24.6 %all_to_all.21 = f32[64,40,128]{2,1,0:T(8,128)S(1)} all-to-all(f32[64,40,128]{2,1,0:T(8,128)S(1)} %broadcast_in_dim.6), channel_id=1, replica_groups={{0,2,4,6,8,10,12,14,16,18,20,22,24,26,28,30,32,34,36,38,40,42,44,46,48,..., dimensions={0} | all-to-all | bytes 2621440 | tf_op jit(solution)/shard_map/all_to_all | solution.py:595
  75.5 3.8 %collective-permute-start.1 = (f32[2560,128]{1,0:T(8,128)S(1)}, f32[2560,128]{1,0:T(8,128)S(1)}, u32[]{:S(2)}, u32[]{:S(2)}) collective-permute-start(f32[2560,128]{1,0:T(8,128)S(1)} %bitcast.11), channel_id=1, source_target_pairs={{0,1},{1,0},{2,3},{3,2},{4,5},{5,4},{6,7},{7,6},{8,9},{9,8},{10,11... | collective-permute-start | bytes 3932168 | tf_op jit(solution)/shard_map/ppermute | solution.py:597
  79.2 2.7 %collective-permute-done.1.other_ref = f32[2560,128]{1,0:T(8,128)S(1)} collective-permute-done((f32[2560,128]{1,0:T(8,128)S(1)}, f32[2560,128]{1,0:T(8,128)S(1)}, u32[]{:S(2)}, u32[]{:S(2)}) %collective-permute-start.1) | collective-permute-done | bytes 1310752 | tf_op jit(solution)/shard_map/ppermute | solution.py:597
  81.9 0.0 copy-start
  81.9 0.0 copy-done.3
  81.9 0.0 copy-done.4
  81.9 14.8 %panel.1 = (f32[32,2048]{1,0:T(8,128)}, f32[512,128]{1,0:T(8,128)}) custom-call(s32[2]{0:T(128)S(1)} %pad_add_fusion.place_ref, f32[2560,128]{1,0:T(8,128)S(1)} %bitcast.12, f32[2560,128]{1,0:T(8,128)S(1)} %collective-permute-done.1.other_ref, f32[1,2048]{1,0:T(1,128)S(1)} %bitcast.17, f32[1,2048]{1,0:T(1,128)S(1)} %bitcast.19, ...), custom_call_target="tpu_custom_call" | custom-call | flops 4194304000 | bytes 16515072 | tf_op jit(solution)/shard_map/panel/pallas_call | solution.py:263
  96.7 0.0 copy-done
  96.7 4.3 %all-to-all-start.2 = ((f32[128,4,128]{2,1,0:T(4,128)}), f32[128,4,128]{2,1,0:T(4,128)S(1)}, u32[]{:S(2)}, u32[]{:S(2)}) async-start(f32[128,4,128]{2,1,0:T(4,128)} %bitcast.8), calls=%async_computation.2 | async-start | bytes 524288 | tf_op jit(solution)/shard_map/all_to_all | solution.py:608
  101.0 32.9 %solve_first.1 = (f32[1152,128]{1,0:T(8,128)S(1)}, f32[512,128]{1,0:T(8,128)S(1)}, f32[864,128]{1,0:T(8,128)S(1)}, f32[736,128]{1,0:T(8,128)S(1)}, f32[608,128]{1,0:T(8,128)S(1)}, /*index=5*/f32[480,128]{1,0:T(8,128)S(1)}) custom-call(s32[2]{0:T(128)S(1)} %pad_add_fusion.place_ref, f32[2560,128]{1,0:T(8,128)S(1)} %bitcast.13, f32[2560,128]{1,0:T(8,128)} %copy-done), custom_call_target="tpu_custom_call" | custom-call | flops 20000000000 | bytes 10000000 | tf_op jit(solution)/shard_map/solve_first/pallas_call | solution.py:534
  133.9 0.0 copy-start.6
  133.9 0.8 copy-done.6
  134.7 0.0 all-to-all-done.2
  134.7 0.1 reduce_sum.19
  134.9 0.7 broadcast_in_dim.7
  135.6 9.8 %all-to-all-start.3 = ((f32[128,4,128]{2,1,0:T(4,128)}), f32[128,4,128]{2,1,0:T(4,128)S(1)}, u32[]{:S(2)}, u32[]{:S(2)}) async-start(f32[128,4,128]{2,1,0:T(4,128)} %broadcast_in_dim.7), calls=%async_computation.3 | async-start | bytes 524288 | tf_op jit(solution)/shard_map/all_to_all | solution.py:612
  145.4 0.0 copy-start.7
  145.4 1.1 copy-done.7
  146.4 0.0 copy-start.1
  146.4 13.4 %solve_second.1 = (f32[96,128]{1,0:T(8,128)S(1)}, f32[384,128]{1,0:T(8,128)S(1)}, f32[352,128]{1,0:T(8,128)S(1)}, f32[224,128]{1,0:T(8,128)S(1)}, f32[96,128]{1,0:T(8,128)S(1)}) custom-call(f32[1152,128]{1,0:T(8,128)S(1)} %copy-done.7), custom_call_target="tpu_custom_call" | custom-call | flops 20000000000 | bytes 10000000 | tf_op jit(solution)/shard_map/solve_second/pallas_call | solution.py:550
  159.9 0.0 all-to-all-done.3
  159.9 0.0 copy-done.1
  159.9 12.9 %solve_last.1 = f32[1,2048]{1,0:T(1,128)} custom-call(f32[96,128]{1,0:T(8,128)S(1)} %get-tuple-element.25.last_ref, f32[512,128]{1,0:T(8,128)S(1)} %get-tuple-element.26.inv0_ref, f32[384,128]{1,0:T(8,128)S(1)} %get-tuple-element.27.inv1_ref, f32[512,128]{1,0:T(8,128)S(1)} %bitcast.14, f32[1,2048]{1,0:T(1,128)S(1)} %bitcast.18, f32[1,2048]{1,0:T(1,128)S(1)} %bitcast.20, ...), custom_call_target="tpu_custom_call" | custom-call | tf_op jit(solution)/shard_map/solve_last/pallas_call | solution.py:567
Async XLA Ops:
  0.7 0.7 copy-start.2
  1.4 0.7 copy-start.5
  15.8 3.9 %collective-permute-start = (f32[2560,128]{1,0:T(8,128)S(1)}, f32[2560,128]{1,0:T(8,128)S(1)}, u32[]{:S(2)}, u32[]{:S(2)}) collective-permute-start(f32[2560,128]{1,0:T(8,128)S(1)} %get-tuple-element.20), channel_id=1, source_target_pairs={{0,1},{1,0},{2,3},{3,2},{4,5},{5,4},{6,7},{7,6},{8,9},{9,8},{10,11... | collective-permute-start | bytes 3932168 | tf_op jit(solution)/shard_map/ppermute | solution.py:592
  50.8 31.1 %copy-start.3 = (f32[2048]{0:T(1024)S(1)}, f32[2048]{0:T(1024)}, u32[]{:S(2)}) copy-start(f32[2048]{0:T(1024)} %param.8) | copy-start | bytes 24580
  50.8 31.1 %copy-start.4 = (f32[2048]{0:T(1024)S(1)}, f32[2048]{0:T(1024)}, u32[]{:S(2)}) copy-start(f32[2048]{0:T(1024)} %param.9) | copy-start | bytes 24580
  75.5 6.4 %collective-permute-start.1 = (f32[2560,128]{1,0:T(8,128)S(1)}, f32[2560,128]{1,0:T(8,128)S(1)}, u32[]{:S(2)}, u32[]{:S(2)}) collective-permute-start(f32[2560,128]{1,0:T(8,128)S(1)} %bitcast.11), channel_id=1, source_target_pairs={{0,1},{1,0},{2,3},{3,2},{4,5},{5,4},{6,7},{7,6},{8,9},{9,8},{10,11... | collective-permute-start | bytes 3932168 | tf_op jit(solution)/shard_map/ppermute | solution.py:597
  81.9 14.8 %copy-start = (f32[2560,128]{1,0:T(8,128)}, f32[2560,128]{1,0:T(8,128)S(1)}, u32[]{:S(2)}) copy-start(f32[2560,128]{1,0:T(8,128)S(1)} %collective-permute-done.1.other_ref) | copy-start | bytes 3932164
  96.7 38.0 %all-to-all-start.2 = ((f32[128,4,128]{2,1,0:T(4,128)}), f32[128,4,128]{2,1,0:T(4,128)S(1)}, u32[]{:S(2)}, u32[]{:S(2)}) async-start(f32[128,4,128]{2,1,0:T(4,128)} %bitcast.8), calls=%async_computation.2 | async-start | bytes 524288 | tf_op jit(solution)/shard_map/all_to_all | solution.py:608
  133.9 0.8 copy-start.6
  135.6 24.3 %all-to-all-start.3 = ((f32[128,4,128]{2,1,0:T(4,128)}), f32[128,4,128]{2,1,0:T(4,128)S(1)}, u32[]{:S(2)}, u32[]{:S(2)}) async-start(f32[128,4,128]{2,1,0:T(4,128)} %broadcast_in_dim.7), calls=%async_computation.3 | async-start | bytes 524288 | tf_op jit(solution)/shard_map/all_to_all | solution.py:612
  145.4 1.1 copy-start.7
  146.4 13.5 %copy-start.1 = (f32[32,2048]{1,0:T(8,128)S(1)}, f32[32,2048]{1,0:T(8,128)}, u32[]{:S(2)}) copy-start(f32[32,2048]{1,0:T(8,128)} %get-tuple-element.21.new_ref) | copy-start | bytes 786436
where the time goes:
time: 175 us; the launch traced here: 173 us
  Pallas kernels  87.8 us (50%)
  blocking collectives  55.4 us (32%)
  starting transfers between devices  19 us (11%)
  waiting for transfers between devices  5.33 us (3%)
  local copies, waits for them, and re-layouts  4.08 us (2%)
    pallas_call x1, Pallas kernels, solve_first(): pl.pallas_call(solve_first_kernel, grid=(1,), out_shape=tuple((shape(r) f...  32.9 us
    all_to_all x1, blocking collectives, sum_large(): parts = lax.all_to_all(keep, AXES, 0, 0, axis_index_groups=SAME_CORE)  30.8 us
    all_to_all x1, blocking collectives, sum_large(): lax.all_to_all(jnp.broadcast_to(part, parts.shape), AXES, 0, 0, axis_inde...  24.6 us
    pallas_call x1, Pallas kernels, panel(): pl.pallas_call(panel_kernel, grid=(ROWS // PANEL_TILE,), out_shape=(jax.S...  14.8 us
    pallas_call x1, Pallas kernels, gram(): pl.pallas_call(gram_kernel, grid=(ROWS // GRAM_TILE,), out_shape=(half, h...  13.8 us
    pallas_call x1, Pallas kernels, solve_second(): pl.pallas_call(solve_second_kernel, grid=(1,), out_shape=tuple((shape(r)...  13.4 us
    pallas_call x1, Pallas kernels, solve_last(): pl.pallas_call(solve_last_kernel, grid=(1,), out_shape=jax.ShapeDtypeStru...  12.9 us
    all_to_all x1, starting transfers between devices, on_device(): lax.all_to_all(jnp.broadcast_to(part, parts.shape), AXES, 0, 0)  9.76 us
  transfers between devices with their start and end apart: 4, of which 2 were waited for; matrix products, arithmetic and copies ran while one was open for 0% of the time, Pallas kernels for 27%

commit v1 on v0

--- a/solution.py
+++ b/solution.py
@@ -47,6 +47,7 @@
 
 NN = ((1,), (0,))
 NT = ((1,), (1,))
+TN = ((0,), (0,))
 
 
 def column(row):
@@ -65,16 +66,15 @@
 GRAM_TILE = 1024
 
 
-def gram_kernel(pivots_ref, place_ref, diag_ref, samples_ref, prev_ref, keep_ref, send_ref, acc_ref, picks_ref, srow_ref, sem):
+def gram_kernel(place_ref, diag_ref, samples_ref, prev_ref, keep_ref, send_ref, acc_ref, picks_ref, srow_ref, sem):
     step = pl.program_id(0)
-    base = place_ref[0]
 
     def row_copy(p):
-        start = pl.multiple_of((pivots_ref[p] - base) // 16 * 16, 16)
+        start = pl.multiple_of(place_ref[2 + p] // 16 * 16, 16)
         return pltpu.make_async_copy(samples_ref.at[pl.ds(start, 16)], srow_ref.at[p], sem.at[p])
 
     def owned(p):
-        place = pivots_ref[p] - base
+        place = place_ref[2 + p]
         return (place >= 0) & (place < ROWS)
 
     @pl.when(step == 0)
@@ -102,7 +102,7 @@
         at += PREV - first
 
     def factor_row(p, carry):
-        place = pivots_ref[p] - base
+        place = place_ref[2 + p]
 
         @pl.when(owned(p) & (place // GRAM_TILE == step))
         def _():
@@ -128,7 +128,7 @@
             def _():
                 row_copy(p).wait()
                 sub = lax.broadcasted_iota(jnp.int32, (16, FEAT), 0)
-                row = jnp.sum(jnp.where(sub == (pivots_ref[p] - base) % 16, srow_ref[p].astype(F32), 0.0), axis=0, keepdims=True)
+                row = jnp.sum(jnp.where(sub == place_ref[2 + p] % 16, srow_ref[p].astype(F32), 0.0), axis=0, keepdims=True)
                 for c in range(FEAT // LANES):
                     picks_ref[pl.ds(c * PANEL + p, 1), :] = row[:, c * LANES : (c + 1) * LANES]
 
@@ -157,14 +157,13 @@
             write((send_ref, keep_ref))
 
 
-def gram(samples, prev_t, pivots, diag, place):
+def gram(samples, prev_t, diag, place):
     half = jax.ShapeDtypeStruct((HALF, LANES), F32)
     return pl.pallas_call(
         gram_kernel,
         grid=(ROWS // GRAM_TILE,),
         out_shape=(half, half),
         in_specs=[
-            pl.BlockSpec(memory_space=pltpu.SMEM),
             pl.BlockSpec(memory_space=pltpu.SMEM),
             pl.BlockSpec((1, GRAM_TILE), lambda i: (0, i)),
             pl.BlockSpec(memory_space=pl.ANY),
@@ -180,7 +179,7 @@
         compiler_params=pltpu.CompilerParams(vmem_limit_bytes=VMEM_LIMIT),
         cost_estimate=pl.CostEstimate(flops=6 * ROWS * RANK * 640, bytes_accessed=ROWS * PREV * 4, transcendentals=0),
         name="gram",
-    )(pivots, place, diag, samples, prev_t)
+    )(place, diag, samples, prev_t)
 
 
 PANEL_TILE = 512
@@ -332,12 +331,21 @@
         cols = inverse8([spread(rows[p], 8 * p + j) for j in range(8)])
         own = jnp.where(inside, jnp.where(lane == sub + 8 * p, 1.0, 0.0), rows[p])
         pivot = tree([cols[j] * jnp.broadcast_to(own[j : j + 1, :], (8, LANES)) for j in range(8)])
-        spread_rows = [jnp.broadcast_to(pivot[j : j + 1, :], (8, LANES)) for j in range(8)]
+        times = jnp.where(inside, 0.0, jnp.where(lane < 8 * p, -rows[p], rows[p]))
+        if p + 1 < n:
+            update = tree([spread(rows[p + 1], 8 * p + j) * jnp.broadcast_to(pivot[j : j + 1, :], (8, LANES)) for j in range(8)])
+            following = jnp.where(inside, 0.0, rows[p + 1]) - update
+        h, m, lo = (x.astype(F32) for x in three(times))
+        ph, pm, plo = (x.astype(F32) for x in three(pivot))
+        left = jnp.concatenate([h, h, m, m, h, lo], axis=0).astype(BF16)
+        right = jnp.concatenate([ph, pm, ph, pm, plo, ph], axis=0).astype(BF16)
+        update = mm(left, right, TN)
+        for q in range(n):
+            if q not in (p, p + 1):
+                rows[q] = jnp.where(inside, 0.0, rows[q]) - update[8 * q : 8 * q + 8]
         rows[p] = pivot
-        for step in range(1, n):
-            q = (p + step) % n
-            update = tree([spread(rows[q], 8 * p + j) * spread_rows[j] for j in range(8)])
-            rows[q] = jnp.where(inside, 0.0, rows[q]) - update
+        if p + 1 < n:
+            rows[p + 1] = following
         yield
     return rows
 
@@ -424,7 +432,8 @@
 LEFT = [PACKED_AT[j] - PACKED_AT[CUTS[1]] for j in range(CUTS[1], NB + 1)]
 
 
-def solve_first_kernel(place_ref, mine_ref, other_ref, left_ref, inv_ref, *refs):
+def solve_first_kernel(place_ref, mine_ref, other_ref, left_ref, inv_ref, token_ref, *refs):
+    token_ref[...] = jnp.zeros_like(token_ref)
     t_refs, a_ref = refs[:-1], refs[-1]
     lane = lax.broadcasted_iota(jnp.int32, (LANES, LANES), 1)
     sub = lax.broadcasted_iota(jnp.int32, (LANES, LANES), 0)
@@ -450,7 +459,7 @@
     eliminate(0, CUTS[1], cols, dict(enumerate(t_refs)), inv_ref)
 
 
-def solve_second_kernel(left_ref, last_ref, inv_ref, *refs):
+def solve_second_kernel(token_ref, left_ref, last_ref, inv_ref, *refs):
     t_refs, a_ref = refs[:-1], refs[-1]
     a_ref[...] = left_ref[...]
     eliminate(CUTS[1], CUTS[2], {j: (a_ref, LEFT[j - CUTS[1]]) for j in range(CUTS[1], NB)}, {CUTS[1] + i: r for i, r in enumerate(t_refs)}, inv_ref)
@@ -511,11 +520,8 @@
     for copy in copies:
         copy.wait()
 
-    def some(i, total):
-        at = pl.multiple_of(i * 32, 32)
-        return total + tree([weigh(prev_ref, at + 8 * j, at + 8 * j) for j in range(4)])
-
-    total = lax.fori_loop(0, PREV // 32, some, total)
+    for i in range(0, PREV, 32):
+        total = total + tree([weigh(prev_ref, i + 8 * j, i + 8 * j) for j in range(4)])
     fw = jnp.sum(total, axis=0, keepdims=True)
     out_ref[...] = diag_ref[...] * rhs_ref[...] - diag_ref[...] * fw
 
@@ -530,7 +536,7 @@
 
 def solve_first(place, mine, other):
     below = [PACKED[k] - LANES for k in range(CUTS[1])]
-    outs = [LEFT[-1], CUTS[1] * LANES] + below
+    outs = [LEFT[-1], CUTS[1] * LANES, 8] + below
     return pl.pallas_call(
         solve_first_kernel,
         grid=(1,),
@@ -544,20 +550,20 @@
     )(place, mine, other)
 
 
-def solve_second(left):
+def solve_second(token, left):
     below = [PACKED[k] - LANES for k in range(CUTS[1], CUTS[2])]
     outs = [PACKED[NB - 1], (CUTS[2] - CUTS[1]) * LANES] + below
     return pl.pallas_call(
         solve_second_kernel,
         grid=(1,),
         out_shape=tuple(shape(r) for r in outs),
-        in_specs=[block_spec(LEFT[-1])],
+        in_specs=[pl.BlockSpec(memory_space=pl.ANY), block_spec(LEFT[-1])],
         out_specs=tuple(block_spec(r) for r in outs),
         scratch_shapes=[pltpu.VMEM((LEFT[-1], LANES), F32)],
         compiler_params=pltpu.CompilerParams(vmem_limit_bytes=VMEM_LIMIT),
         cost_estimate=pl.CostEstimate(flops=2 * 10**10, bytes_accessed=10**7, transcendentals=0),
         name="solve_second",
-    )(left)
+    )(token, left)
 
 
 def solve_last(last, inv0, inv1, ext, t, diag, rhs, new_t, prev_t):
@@ -599,18 +605,18 @@
 
 def on_device(samples, prev_factor, pivots, inv_diag, rhs):
     index = lax.axis_index(AXES)
-    place = jnp.stack([index * ROWS, index % 2]).astype(jnp.int32)
+    place = jnp.concatenate([jnp.stack([index, index % 2]), pivots - index * ROWS]).astype(jnp.int32)
     diag, rhs = inv_diag.reshape(1, ROWS), rhs.reshape(1, ROWS)
     prev_t = prev_factor.T
-    keep, send = gram(samples, prev_t, pivots, diag, place)
+    keep, send = gram(samples, prev_t, diag, place)
     mine, other = sum_large(keep, send)
     new_t, ext = panel(place, mine, other, diag, rhs, samples, prev_t)
     parts = lax.all_to_all(ext.reshape(128, -1, LANES), AXES, 0, 0)
-    left, inv0, *t0 = solve_first(place, mine, other)
-    parts, left = lax.optimization_barrier((parts, left))
+    left, inv0, token, *t0 = solve_first(place, mine, other)
+    parts, token = lax.optimization_barrier((parts, token))
     part = jnp.sum(parts, axis=0)
     ext = lax.all_to_all(jnp.broadcast_to(part, parts.shape), AXES, 0, 0).reshape(ext.shape)
-    last, inv1, *t1 = solve_second(left)
+    last, inv1, *t1 = solve_second(token, left)
     out = solve_last(last, inv0, inv1, ext, t0 + t1, diag, rhs, new_t, prev_t)
     return (new_t.T, out.reshape(ROWS))
 

time: 175 us -> 156 us (0.89)
  Pallas kernels: 87.8 us -> 69.8 us
    pallas_call x1, Pallas kernels: 32.9 us -> 18.7 us  [solve_first(): pl.pallas_call(solve_first_kernel, grid=(1,), out_shape=tuple((shape(r) f...]
    pallas_call x1, Pallas kernels: 12.9 us -> 10.9 us  [solve_last(): pl.pallas_call(solve_last_kernel, grid=(1,), out_shape=jax.ShapeDtypeStru...]
  transfers between devices with their start and end apart: 4 -> 4, of which waited for: 2 -> 2; matrix products, arithmetic and copies ran while one was open for 0% -> 0% of each run, Pallas kernels for 27% -> 20%
where the time goes in v1:
time: 156 us; the launch traced here: 155 us
  Pallas kernels  69.8 us (45%)
  blocking collectives  55.1 us (35%)
  starting transfers between devices  19.8 us (13%)
  waiting for transfers between devices  5.33 us (3%)
  local copies, waits for them, and re-layouts  3.41 us (2%)
    all_to_all x1, blocking collectives, sum_large(): parts = lax.all_to_all(keep, AXES, 0, 0, axis_index_groups=SAME_CORE)  30.5 us
    all_to_all x1, blocking collectives, sum_large(): lax.all_to_all(jnp.broadcast_to(part, parts.shape), AXES, 0, 0, axis_inde...  24.6 us
    pallas_call x1, Pallas kernels, solve_first(): pl.pallas_call(solve_first_kernel, grid=(1,), out_shape=tuple((shape(r) f...  18.7 us
    pallas_call x1, Pallas kernels, panel(): pl.pallas_call(panel_kernel, grid=(ROWS // PANEL_TILE,), out_shape=(jax.S...  14.8 us
    pallas_call x1, Pallas kernels, gram(): pl.pallas_call(gram_kernel, grid=(ROWS // GRAM_TILE,), out_shape=(half, h...  13.4 us
    pallas_call x1, Pallas kernels, solve_second(): pl.pallas_call(solve_second_kernel, grid=(1,), out_shape=tuple((shape(r)...  12.1 us
    pallas_call x1, Pallas kernels, solve_last(): pl.pallas_call(solve_last_kernel, grid=(1,), out_shape=jax.ShapeDtypeStru...  10.9 us
    all_to_all x1, starting transfers between devices, on_device(): lax.all_to_all(jnp.broadcast_to(part, parts.shape), AXES, 0, 0)  9.98 us
  transfers between devices with their start and end apart: 4, of which 2 were waited for; matrix products, arithmetic and copies ran while one was open for 0% of the time, Pallas kernels for 20%

profile of v1, /device:TPU:1, one launch (start us, length us, event | category | flops | bytes accessed | tf_op | source)
XLA Modules:
  0.0 155.5 jit_solution(2078112733992956574)
XLA Ops:
  0.6 0.7 broadcast_subtract_fusion
  1.3 0.1 pad_add_fusion.place_ref
  1.4 0.0 copy-start.2
  1.4 0.7 copy-done.2
  2.1 13.4 %gram.1 = (f32[2560,128]{1,0:T(8,128)S(1)}, f32[2560,128]{1,0:T(8,128)S(1)}) custom-call(s32[34]{0:T(128)S(1)} %pad_add_fusion.place_ref, f32[1,2048]{1,0:T(1,128)S(1)} %bitcast.16, bf16[2048,2048]{1,0:T(8,128)(2,1)} %samples_ref.3, f32[992,2048]{1,0:T(8,128)} %bitcast.21), custom_call_target="tpu_custom_call" | custom-call | flops 8053063680 | bytes 8126464 | tf_op jit(solution)/shard_map/gram/pallas_call | solution.py:162
  15.5 1.8 %collective-permute-start = (f32[2560,128]{1,0:T(8,128)S(1)}, f32[2560,128]{1,0:T(8,128)S(1)}, u32[]{:S(2)}, u32[]{:S(2)}) collective-permute-start(f32[2560,128]{1,0:T(8,128)S(1)} %get-tuple-element.21), channel_id=1, source_target_pairs={{0,1},{1,0},{2,3},{3,2},{4,5},{5,4},{6,7},{7,6},{8,9},{9,8},{10,11... | collective-permute-start | bytes 3932168 | tf_op jit(solution)/shard_map/ppermute | solution.py:598
  17.3 2.7 %collective-permute-done = f32[2560,128]{1,0:T(8,128)S(1)} collective-permute-done((f32[2560,128]{1,0:T(8,128)S(1)}, f32[2560,128]{1,0:T(8,128)S(1)}, u32[]{:S(2)}, u32[]{:S(2)}) %collective-permute-start) | collective-permute-done | bytes 1310752 | tf_op jit(solution)/shard_map/ppermute | solution.py:598
  20.0 0.1 add.12
  20.1 30.5 %all_to_all.20 = f32[64,40,128]{2,1,0:T(8,128)S(1)} all-to-all(f32[64,40,128]{2,1,0:T(8,128)S(1)} %bitcast.24), channel_id=1, replica_groups={{0,2,4,6,8,10,12,14,16,18,20,22,24,26,28,30,32,34,36,38,40,42,44,46,48,..., dimensions={0} | all-to-all | bytes 2621440 | tf_op jit(solution)/shard_map/all_to_all | solution.py:599
  50.6 0.1 reduce_sum.18
  50.7 0.1 broadcast_in_dim.6
  50.8 0.0 copy-start.3
  50.8 0.0 copy-start.4
  50.8 24.6 %all_to_all.21 = f32[64,40,128]{2,1,0:T(8,128)S(1)} all-to-all(f32[64,40,128]{2,1,0:T(8,128)S(1)} %broadcast_in_dim.6), channel_id=1, replica_groups={{0,2,4,6,8,10,12,14,16,18,20,22,24,26,28,30,32,34,36,38,40,42,44,46,48,..., dimensions={0} | all-to-all | bytes 2621440 | tf_op jit(solution)/shard_map/all_to_all | solution.py:601
  75.5 3.8 %collective-permute-start.1 = (f32[2560,128]{1,0:T(8,128)S(1)}, f32[2560,128]{1,0:T(8,128)S(1)}, u32[]{:S(2)}, u32[]{:S(2)}) collective-permute-start(f32[2560,128]{1,0:T(8,128)S(1)} %bitcast.11), channel_id=1, source_target_pairs={{0,1},{1,0},{2,3},{3,2},{4,5},{5,4},{6,7},{7,6},{8,9},{9,8},{10,11... | collective-permute-start | bytes 3932168 | tf_op jit(solution)/shard_map/ppermute | solution.py:603
  79.2 2.7 %collective-permute-done.1.other_ref = f32[2560,128]{1,0:T(8,128)S(1)} collective-permute-done((f32[2560,128]{1,0:T(8,128)S(1)}, f32[2560,128]{1,0:T(8,128)S(1)}, u32[]{:S(2)}, u32[]{:S(2)}) %collective-permute-start.1) | collective-permute-done | bytes 1310752 | tf_op jit(solution)/shard_map/ppermute | solution.py:603
  81.9 0.0 copy-start
  81.9 0.0 copy-done.3
  81.9 0.0 copy-done.4
  81.9 14.8 %panel.1 = (f32[32,2048]{1,0:T(8,128)}, f32[512,128]{1,0:T(8,128)}) custom-call(s32[34]{0:T(128)S(1)} %pad_add_fusion.place_ref, f32[2560,128]{1,0:T(8,128)S(1)} %bitcast.12, f32[2560,128]{1,0:T(8,128)S(1)} %collective-permute-done.1.other_ref, f32[1,2048]{1,0:T(1,128)S(1)} %bitcast.17, f32[1,2048]{1,0:T(1,128)S(1)} %bitcast.19, ...), custom_call_target="tpu_custom_call" | custom-call | flops 4194304000 | bytes 16515072 | tf_op jit(solution)/shard_map/panel/pallas_call | solution.py:262
  96.7 0.0 copy-done
  96.7 4.3 %all-to-all-start.2 = ((f32[128,4,128]{2,1,0:T(4,128)}), f32[128,4,128]{2,1,0:T(4,128)S(1)}, u32[]{:S(2)}, u32[]{:S(2)}) async-start(f32[128,4,128]{2,1,0:T(4,128)} %bitcast.8), calls=%async_computation.2 | async-start | bytes 524288 | tf_op jit(solution)/shard_map/all_to_all | solution.py:614
  100.9 18.7 %solve_first.1 = (f32[1152,128]{1,0:T(8,128)S(1)}, f32[512,128]{1,0:T(8,128)S(1)}, f32[8,128]{1,0:T(8,128)S(1)}, f32[864,128]{1,0:T(8,128)S(1)}, f32[736,128]{1,...) custom-call(s32[34]{0:T(128)S(1)} %pad_add_fusion.place_ref, f32[2560,128]{1,0:T(8,128)S(1)} %bitcast.13, ...), custom_call_target="tpu_custom_call" | custom-call | flops 20000000000 | bytes 10000000 | tf_op jit(solution)/shard_map/solve_first/pallas_call | solution.py:540
  119.6 0.0 copy-start.5
  119.6 0.8 copy-done.5
  120.4 0.0 all-to-all-done.2
  120.4 0.1 reduce_sum.19
  120.6 0.7 broadcast_in_dim.7
  121.3 10.0 %all-to-all-start.3 = ((f32[128,4,128]{2,1,0:T(4,128)}), f32[128,4,128]{2,1,0:T(4,128)S(1)}, u32[]{:S(2)}, u32[]{:S(2)}) async-start(f32[128,4,128]{2,1,0:T(4,128)} %broadcast_in_dim.7), calls=%async_computation.3 | async-start | bytes 524288 | tf_op jit(solution)/shard_map/all_to_all | solution.py:618
  131.3 0.0 copy-start.6
  131.3 1.1 copy-done.6
  132.4 0.0 copy-start.1
  132.4 12.1 %solve_second.1 = (f32[96,128]{1,0:T(8,128)S(1)}, f32[384,128]{1,0:T(8,128)S(1)}, f32[352,128]{1,0:T(8,128)S(1)}, f32[224,128]{1,0:T(8,128)S(1)}, f32[96,128]{1,0:T(8,128)S(1)}) custom-call(f32[8,128]{1,0:T(8,128)S(1)} %get-tuple-element.25.token_ref, f32[1152,128]{1,0:T(8,128)S(1)} %copy-done.6), custom_call_target="tpu_custom_call" | custom-call | flops 20000000000 | bytes 10000000 | tf_op jit(solution)/shard_map/solve_second/pallas_call | solution.py:556
  144.4 0.0 all-to-all-done.3
  144.4 0.0 copy-done.1
  144.4 10.9 %solve_last.1 = f32[1,2048]{1,0:T(1,128)} custom-call(f32[96,128]{1,0:T(8,128)S(1)} %get-tuple-element.27.last_ref, f32[512,128]{1,0:T(8,128)S(1)} %get-tuple-element.28.inv0_ref, f32[384,128]{1,0:T(8,128)S(1)} %get-tuple-element.29.inv1_ref, f32[512,128]{1,0:T(8,128)S(1)} %bitcast.14, f32[1,2048]{1,0:T(1,128)S(1)} %bitcast.18, f32[1,2048]{1,0:T(1,128)S(1)} %bitcast.20, ...), custom_call_target="tpu_custom_call" | custom-call | tf_op jit(solution)/shard_map/solve_last/pallas_call | solution.py:573
Async XLA Ops:
  1.4 0.7 copy-start.2
  15.5 4.5 %collective-permute-start = (f32[2560,128]{1,0:T(8,128)S(1)}, f32[2560,128]{1,0:T(8,128)S(1)}, u32[]{:S(2)}, u32[]{:S(2)}) collective-permute-start(f32[2560,128]{1,0:T(8,128)S(1)} %get-tuple-element.21), channel_id=1, source_target_pairs={{0,1},{1,0},{2,3},{3,2},{4,5},{5,4},{6,7},{7,6},{8,9},{9,8},{10,11... | collective-permute-start | bytes 3932168 | tf_op jit(solution)/shard_map/ppermute | solution.py:598
  50.8 31.1 %copy-start.3 = (f32[2048]{0:T(1024)S(1)}, f32[2048]{0:T(1024)}, u32[]{:S(2)}) copy-start(f32[2048]{0:T(1024)} %param.8) | copy-start | bytes 24580
  50.8 31.1 %copy-start.4 = (f32[2048]{0:T(1024)S(1)}, f32[2048]{0:T(1024)}, u32[]{:S(2)}) copy-start(f32[2048]{0:T(1024)} %param.9) | copy-start | bytes 24580
  75.5 6.4 %collective-permute-start.1 = (f32[2560,128]{1,0:T(8,128)S(1)}, f32[2560,128]{1,0:T(8,128)S(1)}, u32[]{:S(2)}, u32[]{:S(2)}) collective-permute-start(f32[2560,128]{1,0:T(8,128)S(1)} %bitcast.11), channel_id=1, source_target_pairs={{0,1},{1,0},{2,3},{3,2},{4,5},{5,4},{6,7},{7,6},{8,9},{9,8},{10,11... | collective-permute-start | bytes 3932168 | tf_op jit(solution)/shard_map/ppermute | solution.py:603
  81.9 14.8 %copy-start = (f32[2560,128]{1,0:T(8,128)}, f32[2560,128]{1,0:T(8,128)S(1)}, u32[]{:S(2)}) copy-start(f32[2560,128]{1,0:T(8,128)S(1)} %collective-permute-done.1.other_ref) | copy-start | bytes 3932164
  96.7 23.8 %all-to-all-start.2 = ((f32[128,4,128]{2,1,0:T(4,128)}), f32[128,4,128]{2,1,0:T(4,128)S(1)}, u32[]{:S(2)}, u32[]{:S(2)}) async-start(f32[128,4,128]{2,1,0:T(4,128)} %bitcast.8), calls=%async_computation.2 | async-start | bytes 524288 | tf_op jit(solution)/shard_map/all_to_all | solution.py:614
  119.6 0.8 copy-start.5
  121.3 23.1 %all-to-all-start.3 = ((f32[128,4,128]{2,1,0:T(4,128)}), f32[128,4,128]{2,1,0:T(4,128)S(1)}, u32[]{:S(2)}, u32[]{:S(2)}) async-start(f32[128,4,128]{2,1,0:T(4,128)} %broadcast_in_dim.7), calls=%async_computation.3 | async-start | bytes 524288 | tf_op jit(solution)/shard_map/all_to_all | solution.py:618
  131.3 1.1 copy-start.6
  132.4 12.1 %copy-start.1 = (f32[32,2048]{1,0:T(8,128)S(1)}, f32[32,2048]{1,0:T(8,128)}, u32[]{:S(2)}) copy-start(f32[32,2048]{1,0:T(8,128)} %get-tuple-element.22.new_ref) | copy-start | bytes 786436
